TPU v7x, 512 devices: a whole 4x8x8 slice. The times are simulated.
512 devices in a mesh: grp: 16 (over y_lo, z), blk: 32 (over x, y_hi, core).
Axes of the slice: x: 4, y: 8 (y_hi: 4, y_lo: 2; y = y_hi * 2 + y_lo), z: 8, core: 2. Of those that a mesh axis runs over, the one named last changes fastest.
Arguments:
- modes: bfloat16 [3, 256, 32, 128, 128], P(None, None, 'grp', 'blk'), may hold values from -6 to 6
- metric: float32 [3, 32, 128, 128], P(None, 'grp', 'blk'), may hold values from 0.5 to 2
- block_map: int32 [32, 128, 128], P('grp', 'blk'), may hold values from 0 to 15
- flags: int32 [32, 128, 128], P('grp', 'blk'), may hold values from 0 to 2
- region_scale: float32 [16], replicated, may hold values from 0.5 to 2
Outputs:
- tensor: float32 [8, 256, 256], P(None, 'grp', 'blk')
All inputs are finite; a program needn't handle non-finite values.
Results may differ from a plain program's by a relative error of at most 0.0042.
Values may be sent and summed in bfloat16 or wider, within the bound.
A program may use at most 64 MiB of HBM per device.

v0:
```python
import jax
import jax.numpy as jnp
from jax import lax
from jax.sharding import PartitionSpec as P

KS = 8


def with_halo(shard, sides, width):
    edges = {}
    for axis, dim in sides:
        count, length = (lax.axis_size(axis), shard.shape[dim])
        up = [(i, (i + 1) % count) for i in range(count - 1)]
        last = lax.slice_in_dim(shard, length - width, length, axis=dim)
        first = lax.slice_in_dim(shard, 0, width, axis=dim)
        edges[dim] = (
            lax.ppermute(last, axis, up),
            lax.ppermute(first, axis, [(b, a) for a, b in up]),
        )
    done = []
    for _, dim in sides:
        low, high = edges[dim]
        around = [(width, width) if d in done else (0, 0) for d in range(shard.ndim)]
        shard = jnp.concatenate([jnp.pad(low, around), shard, jnp.pad(high, around)], axis=dim)
        done.append(dim)
    return shard


def in_blocks(shard, dim, count):
    shape = shard.shape
    pieces = shard.reshape(*shape[:dim], count, shape[dim] // count, *shape[dim + 1 :])
    return jnp.moveaxis(pieces, dim, 0)


def sent_and_summed(shard, axis, dim):
    count = lax.axis_size(axis)
    pieces = lax.all_to_all(in_blocks(shard, dim, count), axis, 0, 0, tiled=True)
    return jnp.sum(pieces.astype(jnp.float32), axis=0)


def sent_and_summed_2(shard, axis, dim):
    pieces = in_blocks(shard, dim, lax.axis_size(axis))
    arrived = lax.all_to_all(pieces, axis, split_axis=0, concat_axis=0, tiled=True)
    return arrived.sum(axis=0)


def stencil(padded, metric):
    gx = 0.5 * (padded[:, :, 2:, 1:-1, 1:-1] - padded[:, :, :-2, 1:-1, 1:-1]) * metric[0]
    gy = 0.5 * (padded[:, :, 1:-1, 2:, 1:-1] - padded[:, :, 1:-1, :-2, 1:-1]) * metric[1]
    gz = 0.5 * (padded[:, :, 1:-1, 1:-1, 2:] - padded[:, :, 1:-1, 1:-1, :-2]) * metric[2]
    return jnp.stack([gx, gy, gz])


def weights(block_map, flags, region_scale, metric, norm):
    labels = jnp.arange(region_scale.shape[0], dtype=jnp.int32)[:, None, None, None]
    scale = jnp.sum(
        jnp.where(block_map[None] == labels, region_scale[:, None, None, None], jnp.float32(0.0)),
        axis=0,
    )
    fluid = jnp.where(
        flags == 0, jnp.float32(1.0), jnp.where(flags == 1, jnp.float32(0.0), jnp.float32(0.5))
    )
    return scale * fluid * norm / (metric[0] * metric[1] * metric[2])


def local(modes, metric, block_map, flags, region_scale):
    groups = lax.axis_size("grp")
    blocks = lax.axis_size("blk")
    count = modes.shape[1]
    total_cells = modes.shape[2] * groups * modes.shape[3] * blocks * modes.shape[4]
    norm = float(total_cells) ** (-0.5)
    slab = modes[:, :KS]
    rimmed = with_halo(slab, (("grp", 2), ("blk", 3)), 1)
    padded = jnp.pad(rimmed.astype(jnp.float32), ((0, 0), (0, 0), (0, 0), (0, 0), (1, 1)))
    grads = stencil(padded, metric)
    weight = weights(block_map, flags, region_scale, metric, norm).reshape(-1)
    flat = modes.reshape(3, count, -1)
    flat_wide = flat.astype(jnp.float32)
    grads = grads.reshape(3, 3, KS, -1)
    partials = []
    for k in range(KS):
        grad_k = grads[:, :, k]
        mixed = flat_wide[0][None] * grad_k[:, 0][:, None]
        mixed = mixed + flat_wide[1][None] * grad_k[:, 1][:, None]
        mixed = mixed + flat_wide[2][None] * grad_k[:, 2][:, None]
        tested = (weight[None, None] * mixed).astype(jnp.bfloat16)
        partials.append(
            lax.dot_general(
                tested, flat, (((0, 2), (0, 2)), ((), ())), preferred_element_type=jnp.float32
            )
        )
    partial_value = jnp.stack(partials)
    inner = sent_and_summed(partial_value.astype(jnp.bfloat16), "grp", 1)
    result = sent_and_summed_2(inner, "blk", 2)
    return result


def solution(mesh):
    return jax.shard_map(
        local,
        mesh=mesh,
        in_specs=(
            P(None, None, "grp", "blk", None),
            P(None, "grp", "blk", None),
            P("grp", "blk", None),
            P("grp", "blk", None),
            P(),
        ),
        out_specs=P(None, "grp", "blk"),
        check_vma=False,
    )
```

profile of v0, /device:TPU:1, one launch (start us, length us, event | category | flops | bytes accessed | tf_op | source)
XLA Modules:
  0.0 96.1 jit_solution(9673778883454792527)
XLA Ops:
  0.0 0.9 fusion.107
  0.9 5.6 %collective-permute-start = (bf16[3,8,2,1,128]{4,3,2,1,0:T(2,128)(2,1)S(1)}, bf16[3,8,2,1,128]{4,3,2,1,0:T(2,128)(2,1)S(1)}, u32[]{:S(2)}, u32[]{:S(2)}) collective-permute-start(bf16[3,8,2,1,128]{4,3,2,1,0:T(2,128)(2,1)S(1)} %get-tuple-element.10), channel_id=1, source_target_pairs={{0,1},{1,2},{2,3},{3,4},{4,5},{5,6},{6,7},{7,8},{8,9},{9,10},{10,1... | collective-permute-start | bytes 36872 | tf_op jit(solution)/shard_map/ppermute | solution.py:17
  6.5 0.8 fusion.106
  7.3 4.0 %collective-permute-start.1 = (bf16[3,8,1,4,128]{4,3,2,1,0:T(4,128)(2,1)S(1)}, bf16[3,8,1,4,128]{4,3,2,1,0:T(4,128)(2,1)S(1)}, u32[]{:S(2)}, u32[]{:S(2)}) collective-permute-start(bf16[3,8,1,4,128]{4,3,2,1,0:T(4,128)(2,1)S(1)} %get-tuple-element.8), channel_id=1, source_target_pairs={{0,32},{32,64},{64,96},{96,128},{128,160},{160,192},{192,224},{224... | collective-permute-start | bytes 73736 | tf_op jit(solution)/shard_map/ppermute | solution.py:17
  11.3 1.3 %collective-permute-start.2 = (bf16[3,8,1,4,128]{4,3,2,1,0:T(4,128)(2,1)S(1)}, bf16[3,8,1,4,128]{4,3,2,1,0:T(4,128)(2,1)S(1)}, u32[]{:S(2)}, u32[]{:S(2)}) collective-permute-start(bf16[3,8,1,4,128]{4,3,2,1,0:T(4,128)(2,1)S(1)} %get-tuple-element.9), channel_id=1, source_target_pairs={{32,0},{64,32},{96,64},{128,96},{160,128},{192,160},{224,192},{256... | collective-permute-start | bytes 73736 | tf_op jit(solution)/shard_map/ppermute | solution.py:18
  12.6 1.9 %collective-permute-start.3 = (bf16[3,8,2,1,128]{4,3,2,1,0:T(2,128)(2,1)S(1)}, bf16[3,8,2,1,128]{4,3,2,1,0:T(2,128)(2,1)S(1)}, u32[]{:S(2)}, u32[]{:S(2)}) collective-permute-start(bf16[3,8,2,1,128]{4,3,2,1,0:T(2,128)(2,1)S(1)} %get-tuple-element.11), channel_id=1, source_target_pairs={{1,0},{2,1},{3,2},{4,3},{5,4},{6,5},{7,6},{8,7},{9,8},{10,9},{11,1... | collective-permute-start | bytes 36872 | tf_op jit(solution)/shard_map/ppermute | solution.py:18
  14.6 2.8 %reshape.132 = bf16[3,256,1024]{2,1,0:T(8,128)(2,1)S(1)} reshape(bf16[3,256,2,4,128]{4,3,2,1,0:T(4,128)(2,1)} %param.5) | data formatting | bytes 3145728 | tf_op jit(solution)/shard_map/reshape | solution.py:77
  17.5 1.8 %fusion.105 = (f32[1,256,1024]{2,1,0:T(8,128)}, f32[1,256,1024]{2,1,0:T(8,128)}, f32[1,256,1024]{2,1,0:T(8,128)}) fusion(bf16[3,256,1024]{2,1,0:T(8,128)(2,1)S(1)} %reshape.132), kind=kLoop, calls=%fused_computation.161 | loop fusion | bytes 6291456 | tf_op jit(solution)/shard_map/slice | solution.py:83
  19.4 0.4 copy-done
  19.7 2.3 %reshape.134 = bf16[3,256,1024,1]{2,1,0,3:T(8,128)(2,1)} reshape(bf16[3,256,2,4,128]{4,3,2,1,0:T(4,128)(2,1)S(1)} %copy-done) | data formatting | bytes 3145728 | tf_op jit(solution)/shard_map/reshape | solution.py:77
  24.2 2.7 %fusion.95 = bf16[8,16,16,256]{3,2,1,0:T(8,128)(2,1)S(1)} fusion(bf16[3,256,1024,1]{2,1,0,3:T(8,128)(2,1)S(1)} %copy-done.1, f32[3,1024]{1,0:T(4,128)S(1)} %bitcast.247, f32[16,16,1024]{2,1,0:T(8,128)} %bitcast.239, f32[3,1024]{1,0:T(4,128)S(1)} %bitcast.248, f32[16,16,1024]{2,1,0:T(8,128)} %bitcast.231, f32[3,1024]{1,0:T(4,128)S(1)} %bitcast.249, ...), kind=kOutput, calls=%fused_computation.104 | convolution fusion | flops 408223744 | bytes 4890624 | tf_op jit(solution)/shard_map/dot_general | solution.py:88
  26.9 1.1 %fusion.93 = bf16[8,16,16,256]{3,2,1,0:T(8,128)(2,1)S(1)} fusion(bf16[8,16,16,256]{3,2,1,0:T(8,128)(2,1)S(1)} %fusion.95, bf16[3,256,1024,1]{2,1,0,3:T(8,128)(2,1)S(1)} %copy-done.1, f32[3,1024]{1,0:T(4,128)S(1)} %bitcast.250, f32[3,1024]{1,0:T(4,128)S(1)} %bitcast.251, f32[3,1024]{1,0:T(4,128)S(1)} %bitcast.252, f32[16,16,1024]{2,1,0:T(8,128)S(1)} %bitcast.240, ...), kind=kOutput, calls=%fused_computation.102 | convolution fusion | flops 408223744 | bytes 4902912 | tf_op jit(solution)/shard_map/dot_general | solution.py:88
  28.1 1.1 %fusion.91 = bf16[8,16,16,256]{3,2,1,0:T(8,128)(2,1)S(1)} fusion(bf16[8,16,16,256]{3,2,1,0:T(8,128)(2,1)S(1)} %fusion.93, bf16[3,256,1024,1]{2,1,0,3:T(8,128)(2,1)S(1)} %copy-done.1, f32[3,1024]{1,0:T(4,128)S(1)} %bitcast.253, f32[3,1024]{1,0:T(4,128)S(1)} %bitcast.254, f32[3,1024]{1,0:T(4,128)S(1)} %bitcast.255, f32[16,16,1024]{2,1,0:T(8,128)S(1)} %bitcast.241, ...), kind=kOutput, calls=%fused_computation.100 | convolution fusion | flops 408223744 | bytes 4902912 | tf_op jit(solution)/shard_map/dot_general | solution.py:88
  29.2 1.1 %fusion.89 = bf16[8,16,16,256]{3,2,1,0:T(8,128)(2,1)S(1)} fusion(bf16[8,16,16,256]{3,2,1,0:T(8,128)(2,1)S(1)} %fusion.91, bf16[3,256,1024,1]{2,1,0,3:T(8,128)(2,1)S(1)} %copy-done.1, f32[3,1024]{1,0:T(4,128)S(1)} %bitcast.256, f32[3,1024]{1,0:T(4,128)S(1)} %bitcast.257, f32[3,1024]{1,0:T(4,128)S(1)} %bitcast.258, f32[16,16,1024]{2,1,0:T(8,128)S(1)} %bitcast.242, ...), kind=kOutput, calls=%fused_computation.98 | convolution fusion | flops 408223744 | bytes 4902912 | tf_op jit(solution)/shard_map/dot_general | solution.py:88
  30.3 1.1 %fusion.87 = bf16[8,16,16,256]{3,2,1,0:T(8,128)(2,1)S(1)} fusion(bf16[8,16,16,256]{3,2,1,0:T(8,128)(2,1)S(1)} %fusion.89, bf16[3,256,1024,1]{2,1,0,3:T(8,128)(2,1)S(1)} %copy-done.1, f32[3,1024]{1,0:T(4,128)S(1)} %bitcast.259, f32[3,1024]{1,0:T(4,128)S(1)} %bitcast.260, f32[3,1024]{1,0:T(4,128)S(1)} %bitcast.261, f32[16,16,1024]{2,1,0:T(8,128)S(1)} %bitcast.243, ...), kind=kOutput, calls=%fused_computation.96 | convolution fusion | flops 408223744 | bytes 4902912 | tf_op jit(solution)/shard_map/dot_general | solution.py:88
  31.4 1.1 %fusion.85 = bf16[8,16,16,256]{3,2,1,0:T(8,128)(2,1)S(1)} fusion(bf16[8,16,16,256]{3,2,1,0:T(8,128)(2,1)S(1)} %fusion.87, bf16[3,256,1024,1]{2,1,0,3:T(8,128)(2,1)S(1)} %copy-done.1, f32[3,1024]{1,0:T(4,128)S(1)} %bitcast.262, f32[3,1024]{1,0:T(4,128)S(1)} %bitcast.263, f32[3,1024]{1,0:T(4,128)S(1)} %bitcast.264, f32[16,16,1024]{2,1,0:T(8,128)S(1)} %bitcast.244, ...), kind=kOutput, calls=%fused_computation.94 | convolution fusion | flops 408223744 | bytes 4902912 | tf_op jit(solution)/shard_map/dot_general | solution.py:88
  32.6 1.1 %fusion.83 = bf16[8,16,16,256]{3,2,1,0:T(8,128)(2,1)S(1)} fusion(bf16[8,16,16,256]{3,2,1,0:T(8,128)(2,1)S(1)} %fusion.85, bf16[3,256,1024,1]{2,1,0,3:T(8,128)(2,1)S(1)} %copy-done.1, f32[3,1024]{1,0:T(4,128)S(1)} %bitcast.265, f32[3,1024]{1,0:T(4,128)S(1)} %bitcast.266, f32[3,1024]{1,0:T(4,128)S(1)} %bitcast.267, f32[16,16,1024]{2,1,0:T(8,128)S(1)} %bitcast.245, ...), kind=kOutput, calls=%fused_computation.92 | convolution fusion | flops 408223744 | bytes 4902912 | tf_op jit(solution)/shard_map/dot_general | solution.py:88
  33.7 1.1 %fusion.81 = bf16[8,16,16,256]{3,2,1,0:T(8,128)(2,1)S(1)} fusion(bf16[8,16,16,256]{3,2,1,0:T(8,128)(2,1)S(1)} %fusion.83, bf16[3,256,1024,1]{2,1,0,3:T(8,128)(2,1)S(1)} %copy-done.1, f32[3,1024]{1,0:T(4,128)S(1)} %bitcast.268, f32[3,1024]{1,0:T(4,128)S(1)} %bitcast.269, f32[3,1024]{1,0:T(4,128)S(1)} %bitcast.270, f32[16,16,1024]{2,1,0:T(8,128)S(1)} %bitcast.246, ...), kind=kOutput, calls=%fused_computation.90 | convolution fusion | flops 408223744 | bytes 4902912 | tf_op jit(solution)/shard_map/dot_general | solution.py:88
  34.9 36.6 %all_to_all.10 = bf16[16,8,16,256]{3,2,1,0:T(8,128)(2,1)S(1)} all-to-all(bf16[16,8,16,256]{3,2,1,0:T(8,128)(2,1)S(1)} %copy.10), channel_id=1, replica_groups=mesh['grp'=16,'blk'=32] {'grp'}, dimensions={0} | all-to-all | bytes 2097152 | tf_op jit(solution)/shard_map/all_to_all | solution.py:37
  72.1 0.4 reshape.144
  72.5 21.0 %all_to_all.11 = f32[32,1,1024]{2,1,0:T(1,128)S(1)} all-to-all(f32[32,1,1024]{2,1,0:T(1,128)S(1)} %reshape.144), channel_id=1, replica_groups=mesh['grp'=16,'blk'=32] {'blk'}, dimensions={0} | all-to-all | bytes 262144 | tf_op jit(solution)/shard_map/all_to_all | solution.py:43
  93.6 0.5 broadcast.139
  94.1 0.9 reduce
  95.4 0.7 bitcast_reduce_fusion
  (76 shorter events, 3.0 us)
Async XLA Ops:
  0.9 21.2 %collective-permute-start = (bf16[3,8,2,1,128]{4,3,2,1,0:T(2,128)(2,1)S(1)}, bf16[3,8,2,1,128]{4,3,2,1,0:T(2,128)(2,1)S(1)}, u32[]{:S(2)}, u32[]{:S(2)}) collective-permute-start(bf16[3,8,2,1,128]{4,3,2,1,0:T(2,128)(2,1)S(1)} %get-tuple-element.10), channel_id=1, source_target_pairs={{0,1},{1,2},{2,3},{3,4},{4,5},{5,6},{6,7},{7,8},{8,9},{9,10},{10,1... | collective-permute-start | bytes 36872 | tf_op jit(solution)/shard_map/ppermute | solution.py:17
  7.3 14.8 %collective-permute-start.1 = (bf16[3,8,1,4,128]{4,3,2,1,0:T(4,128)(2,1)S(1)}, bf16[3,8,1,4,128]{4,3,2,1,0:T(4,128)(2,1)S(1)}, u32[]{:S(2)}, u32[]{:S(2)}) collective-permute-start(bf16[3,8,1,4,128]{4,3,2,1,0:T(4,128)(2,1)S(1)} %get-tuple-element.8), channel_id=1, source_target_pairs={{0,32},{32,64},{64,96},{96,128},{128,160},{160,192},{192,224},{224... | collective-permute-start | bytes 73736 | tf_op jit(solution)/shard_map/ppermute | solution.py:17
  11.3 10.8 %collective-permute-start.2 = (bf16[3,8,1,4,128]{4,3,2,1,0:T(4,128)(2,1)S(1)}, bf16[3,8,1,4,128]{4,3,2,1,0:T(4,128)(2,1)S(1)}, u32[]{:S(2)}, u32[]{:S(2)}) collective-permute-start(bf16[3,8,1,4,128]{4,3,2,1,0:T(4,128)(2,1)S(1)} %get-tuple-element.9), channel_id=1, source_target_pairs={{32,0},{64,32},{96,64},{128,96},{160,128},{192,160},{224,192},{256... | collective-permute-start | bytes 73736 | tf_op jit(solution)/shard_map/ppermute | solution.py:18
  12.6 4.8 %copy-start.5 = (f32[3,2,4,128]{3,2,1,0:T(4,128)S(1)}, f32[3,2,4,128]{3,2,1,0:T(4,128)}, u32[]{:S(2)}) copy-start(f32[3,2,4,128]{3,2,1,0:T(4,128)} %param.6) | copy-start | bytes 36868
  12.6 9.4 %collective-permute-start.3 = (bf16[3,8,2,1,128]{4,3,2,1,0:T(2,128)(2,1)S(1)}, bf16[3,8,2,1,128]{4,3,2,1,0:T(2,128)(2,1)S(1)}, u32[]{:S(2)}, u32[]{:S(2)}) collective-permute-start(bf16[3,8,2,1,128]{4,3,2,1,0:T(2,128)(2,1)S(1)} %get-tuple-element.11), channel_id=1, source_target_pairs={{1,0},{2,1},{3,2},{4,3},{5,4},{6,5},{7,6},{8,7},{9,8},{10,9},{11,1... | collective-permute-start | bytes 36872 | tf_op jit(solution)/shard_map/ppermute | solution.py:18
  17.4 1.8 %copy-start.6 = (s32[2,4,128]{2,1,0:T(4,128)S(1)}, s32[2,4,128]{2,1,0:T(4,128)}, u32[]{:S(2)}) copy-start(s32[2,4,128]{2,1,0:T(4,128)} %param.7) | copy-start | bytes 12292
  17.4 1.8 %copy-start.8 = (f32[16]{0:T(128)S(1)}, f32[16]{0:T(128)}, u32[]{:S(2)}) copy-start(f32[16]{0:T(128)} %param.9) | copy-start | bytes 196
  17.5 1.9 %copy-start.7 = (s32[2,4,128]{2,1,0:T(4,128)S(1)}, s32[2,4,128]{2,1,0:T(4,128)}, u32[]{:S(2)}) copy-start(s32[2,4,128]{2,1,0:T(4,128)} %param.8) | copy-start | bytes 12292
  17.5 2.3 %copy-start = (bf16[3,256,2,4,128]{4,3,2,1,0:T(4,128)(2,1)S(1)}, bf16[3,256,2,4,128]{4,3,2,1,0:T(4,128)(2,1)}, u32[]{:S(2)}) copy-start(bf16[3,256,2,4,128]{4,3,2,1,0:T(4,128)(2,1)} %param.5) | copy-start | bytes 4718596
  19.7 2.4 %slice-start = ((bf16[3,256,2,4,128]{4,3,2,1,0:T(4,128)(2,1)}), bf16[3,8,2,4,128]{4,3,2,1,0:T(4,128)(2,1)S(1)}, s32[]{:S(2)}) async-start(bf16[3,256,2,4,128]{4,3,2,1,0:T(4,128)(2,1)} %param.5), calls=%async_computation.2 | async-start | bytes 98304 | tf_op jit(solution)/shard_map/slice | solution.py:72
  22.5 1.4 %copy-start.1 = (bf16[3,256,1024,1]{2,1,0,3:T(8,128)(2,1)S(1)}, bf16[3,256,1024,1]{2,1,0,3:T(8,128)(2,1)}, u32[]{:S(2)}) copy-start(bf16[3,256,1024,1]{2,1,0,3:T(8,128)(2,1)} %reshape.134) | copy-start | bytes 4718596
  22.6 1.7 %copy-start.2 = (f32[1,256,1024]{2,1,0:T(8,128)S(1)}, f32[1,256,1024]{2,1,0:T(8,128)}, u32[]{:S(2)}) copy-start(f32[1,256,1024]{2,1,0:T(8,128)} %get-tuple-element.5) | copy-start | bytes 3145732
  24.2 2.7 %copy-start.3 = (f32[1,256,1024]{2,1,0:T(8,128)S(1)}, f32[1,256,1024]{2,1,0:T(8,128)}, u32[]{:S(2)}) copy-start(f32[1,256,1024]{2,1,0:T(8,128)} %get-tuple-element.6) | copy-start | bytes 3145732
  24.2 2.7 %copy-start.4 = (f32[1,256,1024]{2,1,0:T(8,128)S(1)}, f32[1,256,1024]{2,1,0:T(8,128)}, u32[]{:S(2)}) copy-start(f32[1,256,1024]{2,1,0:T(8,128)} %get-tuple-element.7) | copy-start | bytes 3145732
where the time goes:
time: 96.6 us; the launch traced here: 96.1 us
  blocking collectives  57.6 us (60%)
  starting transfers between devices  12.8 us (13%)
  local copies, waits for them, and re-layouts  12.3 us (13%)
  matrix products  10.5 us (11%)
  other arithmetic  2.21 us (2%)
    all_to_all x1, blocking collectives, sent_and_summed(): lax.all_to_all(in_blocks(shard, dim, count), axis, 0, 0, tiled=True)  36.6 us
    all_to_all x1, blocking collectives, sent_and_summed_2(): lax.all_to_all(pieces, axis, split_axis=0, concat_axis=0, tiled=True)  21 us
    dot_general x8, matrix products, local(): lax.dot_general(tested, flat, (((0, 2), (0, 2)), ((), ())), preferred_ele...  10.5 us
    ppermute x2, starting transfers between devices, with_halo(): lax.ppermute(last, axis, up)  9.6 us
    reshape x2, local copies, waits for them, and re-layouts, local(): flat = modes.reshape(3, count, -1)  5.16 us
    ppermute x2, starting transfers between devices, with_halo(): lax.ppermute(first, axis, [(b, a) for a, b in up])  3.21 us
    unnamed x51, local copies, waits for them, and re-layouts  2.17 us
    slice x9, local copies, waits for them, and re-layouts, local(): mixed = flat_wide[0][None] * grad_k[:, 0][:, None]  2 us
  transfers between devices with their start and end apart: 4, of which 0 were waited for; matrix products, arithmetic and copies ran while one was open for 8% of the time, Pallas kernels for 0%

commit v1 on v0

v1 whole, which is shorter than its diff:
```python
import functools

import jax
import jax.numpy as jnp
from jax import lax
from jax.experimental import pallas as pl
from jax.experimental.pallas import tpu as pltpu
from jax.sharding import PartitionSpec as P

KS = 8
M = 256
CELLS = 8
NX, NY = 2, 4
F32, BF16 = jnp.float32, jnp.bfloat16
MESH = pl.DeviceIdType.MESH
BLOCKS = 4


def kernel(
    norm,
    modes_hbm, metric_hbm, map_hbm, flags_hbm, scale_ref,
    out_ref,
    nat, natf, slab, slabf, met, bmap, flg, gtab, bmat, pacc,
    hx_send, hy_send, hx_recv, hy_recv,
    c_send, c_recv, x_send, x_recv, y_send, y_recv, z_send, z_recv, own,
    in_sem, h_ssem, h_rsem, c_ssem, c_rsem, x_ssem, x_rsem, y_ssem, y_rsem, z_ssem, z_rsem,
):
    grp = lax.axis_index("grp")
    blk = lax.axis_index("blk")
    z, y_lo = grp % 8, grp // 8
    core, y_hi, x = blk % 2, (blk // 2) % 4, blk // 8

    def at(dx=0, dyh=0, dyl=0, dz=0, dc=0):
        g = ((y_lo + dyl) % 2) * 8 + (z + dz) % 8
        b = ((x + dx) % 4) * 8 + ((y_hi + dyh) % 4) * 2 + (core + dc) % 2
        return (g, b)

    halo_to = [
        ((grp + 1) % 16, blk),
        ((grp + 15) % 16, blk),
        (grp, (blk + 1) % 32),
        (grp, (blk + 31) % 32),
    ]
    yrel = [(s, t) for s in range(4) for t in range(2)]
    partners = list(halo_to)
    partners.append(at(dc=1))
    partners += [at(dx=r) for r in range(1, 4)]
    partners += [at(dyh=s, dyl=t) for s, t in yrel[1:]]
    partners += [at(dz=q) for q in range(1, 8)]

    barrier = pltpu.get_barrier_semaphore()
    for p in partners:
        pl.semaphore_signal(barrier, inc=1, device_id=p, device_id_type=MESH)

    loads = [
        pltpu.make_async_copy(modes_hbm.at[:, pl.ds(0, KS * CELLS), :], slab, in_sem.at[0]),
        pltpu.make_async_copy(metric_hbm, met, in_sem.at[1]),
        pltpu.make_async_copy(map_hbm, bmap, in_sem.at[2]),
        pltpu.make_async_copy(flags_hbm, flg, in_sem.at[3]),
        pltpu.make_async_copy(modes_hbm, nat, in_sem.at[4]),
    ]
    for c in loads:
        c.start()

    loads[0].wait()
    for c in range(3):
        slabf[c * 64:(c + 1) * 64, :] = slab[c].astype(F32)

    def tile(c, row):
        return slabf[pl.ds(c * 64 + row, KS, stride=CELLS), :]

    s = {(c, row): tile(c, row) for c in range(3) for row in range(CELLS)}
    for side, xi in ((0, 1), (1, 0)):
        for c in range(3):
            for yp in range(2):
                a = s[c, xi * NY + 2 * yp]
                b = s[c, xi * NY + 2 * yp + 1]
                at_row = (c * 2 + yp) * 16
                hx_send[side, at_row:at_row + 16, :] = jnp.concatenate([a, b], 0).astype(BF16)
    for side, yi in ((0, 3), (1, 0)):
        for c in range(3):
            a, b = s[c, yi], s[c, NY + yi]
            hy_send[side, c * 16:c * 16 + 16, :] = jnp.concatenate([a, b], 0).astype(BF16)

    pl.semaphore_wait(barrier, len(partners))

    def remote(src, dst, ssem, rsem, to):
        return pltpu.make_async_remote_copy(
            src_ref=src, dst_ref=dst, send_sem=ssem, recv_sem=rsem,
            device_id=to, device_id_type=MESH,
        )

    halo = []
    for n in range(4):
        src, dst = (hx_send, hx_recv) if n < 2 else (hy_send, hy_recv)
        halo.append(remote(src.at[n % 2], dst.at[n % 2], h_ssem.at[n], h_rsem.at[n], halo_to[n]))
        halo[-1].start()

    loads[1].wait()
    loads[2].wait()
    loads[3].wait()
    region = bmap[...]
    scale = jnp.zeros((CELLS, 128), F32)
    for r in range(16):
        scale = jnp.where(region == r, scale_ref[r], scale)
    kinds = flg[...]
    fluid = jnp.where(kinds == 0, F32(1.0), jnp.where(kinds == 1, F32(0.0), F32(0.5)))
    m = [met[d * CELLS:(d + 1) * CELLS, :] for d in range(3)]
    weight = scale * fluid * norm / (m[0] * m[1] * m[2])
    half = [0.5 * weight * m[d] for d in range(3)]

    loads[4].wait()

    def widen(n, _):
        rows = pl.ds(pl.multiple_of(n * 256, 256), 256)
        for c in range(3):
            natf[c, rows, :] = nat[c, rows, :].astype(F32)
        return 0

    lax.fori_loop(0, 8, widen, 0)

    def spread(n, _):
        cc = (core + n // 4) % 2
        xx = (x + n % 4) % 4
        for pair in range(2):
            starts = []
            for e in range(2):
                yy = (y_hi + 2 * pair + e) % 4
                starts.append((xx * 8 + yy * 2 + cc) * (8 * CELLS))
            rows = pl.ds(pl.multiple_of(n * 32 + pair * 16, 16), 16)
            for d in range(3):
                for row in range(CELLS):
                    both = jnp.concatenate(
                        [natf[d, pl.ds(st + row, 8, stride=CELLS), :] for st in starts], 0
                    )
                    col = (row // 2) * 768 + d * 256 + (row % 2) * 128
                    bmat[rows, col:col + 128] = both.astype(BF16)
        return 0

    lax.fori_loop(0, 8, spread, 0)

    lane = lax.broadcasted_iota(jnp.int32, (KS, 128), 1)

    def put(d, c, row, diff):
        base = (d * 3 + c) * KS
        gtab[row, base:base + KS, :] = diff * half[d][row:row + 1, :]

    for c in range(3):
        for row in range(CELLS):
            v = s[c, row]
            after = jnp.where(lane == 127, F32(0.0), pltpu.roll(v, 127, 1))
            before = jnp.where(lane == 0, F32(0.0), pltpu.roll(v, 1, 1))
            put(2, c, row, after - before)

    for h in halo:
        h.wait_recv()
    keep = [
        jnp.where(grp > 0, F32(1.0), F32(0.0)),
        jnp.where(grp < 15, F32(1.0), F32(0.0)),
        jnp.where(blk > 0, F32(1.0), F32(0.0)),
        jnp.where(blk < 31, F32(1.0), F32(0.0)),
    ]
    for c in range(3):
        xs = [[None] * NY, [None] * NY]
        for side in range(2):
            for yp in range(2):
                at_row = (c * 2 + yp) * 16
                both = hx_recv[side, at_row:at_row + 16, :].astype(F32) * keep[side]
                xs[side][2 * yp], xs[side][2 * yp + 1] = both[:8], both[8:]
        ys = []
        for side in range(2):
            both = hy_recv[side, c * 16:c * 16 + 16, :].astype(F32) * keep[2 + side]
            ys.append((both[:8], both[8:]))
        for xi in range(NX):
            for yi in range(NY):
                row = xi * NY + yi
                hi = s[c, row + NY] if xi == 0 else xs[1][yi]
                lo = s[c, row - NY] if xi == 1 else xs[0][yi]
                put(0, c, row, hi - lo)
                hi = s[c, row + 1] if yi < NY - 1 else ys[1][xi]
                lo = s[c, row - 1] if yi > 0 else ys[0][xi]
                put(1, c, row, hi - lo)

    def compute(b):
        bases = []
        for t in range(2):
            for e in range(2):
                g = ((y_lo + t) % 2) * 8 + (z + 2 * b + e) % 8
                bases.append(g * (16 * CELLS))

        def rows_of(pair, d):
            halves = []
            for e in range(2):
                row = pair * 2 + e
                a = [
                    [natf[c, pl.ds(st + row, 16, stride=CELLS), :] for st in bases]
                    for c in range(3)
                ]
                a = [jnp.concatenate(v, 0) for v in a]
                per_k = []
                for k in range(KS):
                    g = [gtab[row, pl.ds((d * 3 + c) * KS + k, 1), :] for c in range(3)]
                    per_k.append((a[0] * g[0] + a[1] * g[1] + a[2] * g[2]).astype(BF16))
                halves.append(
                    jnp.concatenate(
                        [per_k[k][p * 16:p * 16 + 16] for p in range(4) for k in range(KS)], 0
                    )
                )
            return jnp.concatenate(halves, 1)

        def step(pair, _):
            total = None
            for d in range(3):
                tested = rows_of(pair, d)
                cols = pl.ds(pl.multiple_of(pair * 768 + d * 256, 256), 256)
                part = lax.dot_general(
                    bmat[:, cols], tested, (((1,), (1,)), ((), ())),
                    preferred_element_type=F32,
                )
                total = part if total is None else total + part
            pacc[b] = total + pacc[b]
            return 0

        pacc[b] = jnp.zeros((M, 512), F32)
        lax.fori_loop(0, 4, step, 0)

    sent = []

    def send(*args):
        c = remote(*args)
        c.start()
        sent.append(c)

    def send_core(b):
        c_send[b] = pacc[b, 128:256, :].astype(BF16)
        send(c_send.at[b], c_recv.at[b], c_ssem.at[b], c_rsem.at[b], at(dc=1))

    def arrived(dst, sem):
        pltpu.make_async_copy(dst, dst, sem).wait()

    def send_x(b):
        arrived(c_recv.at[b], c_rsem.at[b])
        for r in (2, 1, 3, 0):
            rows = slice(r * 32, r * 32 + 32)
            v = pacc[b, rows, :] + c_recv[b, rows, :].astype(F32)
            if r == 0:
                pacc[b, rows, :] = v
            else:
                x_send[b, r] = v.astype(BF16)
                send(x_send.at[b, r], x_recv.at[b, r], x_ssem.at[b, r], x_rsem.at[b, r], at(dx=r))

    def send_y(b):
        v = pacc[b, 0:32, :]
        for r in range(1, 4):
            arrived(x_recv.at[b, r], x_rsem.at[b, r])
            v = v + x_recv[b, r].astype(F32)
        for n, (sy, t) in reversed(list(enumerate(yrel))):
            two = [v[sy * 8:sy * 8 + 8, t * 256 + e * 128:t * 256 + e * 128 + 128] for e in range(2)]
            both = jnp.concatenate(two, 0)
            if n == 0:
                own[b] = both
            else:
                y_send[b, n] = both.astype(BF16)
                send(
                    y_send.at[b, n], y_recv.at[b, n], y_ssem.at[b, n], y_rsem.at[b, n],
                    at(dyh=sy, dyl=t),
                )

    def send_z(b):
        v = own[b]
        for n in range(1, 8):
            arrived(y_recv.at[b, n], y_rsem.at[b, n])
            v = v + y_recv[b, n].astype(F32)
        for e in range(2):
            q = 2 * b + e
            z_send[q] = v[e * 8:e * 8 + 8]
            if q:
                send(z_send.at[q], z_recv.at[q], z_ssem.at[q], z_rsem.at[q], at(dz=q))

    for b in range(BLOCKS + 3):
        if b < BLOCKS:
            compute(b)
            send_core(b)
        if 0 <= b - 1 < BLOCKS:
            send_x(b - 1)
        if 0 <= b - 2 < BLOCKS:
            send_y(b - 2)
        if 0 <= b - 3 < BLOCKS:
            send_z(b - 3)

    v = z_send[0]
    for q in range(1, 8):
        arrived(z_recv.at[q], z_rsem.at[q])
        v = v + z_recv[q]
    out_ref[...] = v

    for h in halo:
        h.wait_send()
    for c in sent:
        c.wait_send()


def local(modes, metric, block_map, flags, region_scale):
    total_cells = (
        modes.shape[2] * lax.axis_size("grp") * modes.shape[3] * lax.axis_size("blk") * modes.shape[4]
    )
    norm = float(total_cells) ** (-0.5)
    hbm = pl.BlockSpec(memory_space=pl.ANY)
    dma = pltpu.SemaphoreType.DMA
    scratch = [
        pltpu.VMEM((3, M * CELLS, 128), BF16),
        pltpu.VMEM((3, M * CELLS, 128), F32),
        pltpu.VMEM((3, KS * CELLS, 128), BF16),
        pltpu.VMEM((3 * KS * CELLS, 128), F32),
        pltpu.VMEM((3 * CELLS, 128), F32),
        pltpu.VMEM((CELLS, 128), jnp.int32),
        pltpu.VMEM((CELLS, 128), jnp.int32),
        pltpu.VMEM((CELLS, 9 * KS, 128), F32),
        pltpu.VMEM((M, 3072), BF16),
        pltpu.VMEM((BLOCKS, M, 512), F32),
        pltpu.VMEM((2, 96, 128), BF16),
        pltpu.VMEM((2, 48, 128), BF16),
        pltpu.VMEM((2, 96, 128), BF16),
        pltpu.VMEM((2, 48, 128), BF16),
        pltpu.VMEM((BLOCKS, 128, 512), BF16),
        pltpu.VMEM((BLOCKS, 128, 512), BF16),
        pltpu.VMEM((BLOCKS, 4, 32, 512), BF16),
        pltpu.VMEM((BLOCKS, 4, 32, 512), BF16),
        pltpu.VMEM((BLOCKS, 8, 16, 128), BF16),
        pltpu.VMEM((BLOCKS, 8, 16, 128), BF16),
        pltpu.VMEM((8, 8, 128), F32),
        pltpu.VMEM((8, 8, 128), F32),
        pltpu.VMEM((BLOCKS, 16, 128), F32),
        dma((5,)),
        dma((4,)),
        dma((4,)),
        dma((BLOCKS,)),
        dma((BLOCKS,)),
        dma((BLOCKS, 4)),
        dma((BLOCKS, 4)),
        dma((BLOCKS, 8)),
        dma((BLOCKS, 8)),
        dma((8,)),
        dma((8,)),
    ]
    summed = pl.pallas_call(
        functools.partial(kernel, norm),
        out_shape=jax.ShapeDtypeStruct((8, 128), F32),
        in_specs=[hbm, hbm, hbm, hbm, pl.BlockSpec(memory_space=pltpu.SMEM)],
        out_specs=pl.BlockSpec(memory_space=pltpu.VMEM),
        scratch_shapes=scratch,
        compiler_params=pltpu.CompilerParams(
            collective_id=0, has_side_effects=True, vmem_limit_bytes=40 * 1024 * 1024
        ),
        cost_estimate=pl.CostEstimate(
            flops=2 * 2048 * 3072 * 256, bytes_accessed=2 * 1024 * 1024, transcendentals=0
        ),
    )(
        modes.reshape(3, M * CELLS, 128),
        metric.reshape(3 * CELLS, 128),
        block_map.reshape(CELLS, 128),
        flags.reshape(CELLS, 128),
        region_scale,
    )
    return summed.reshape(8, KS, 16).transpose(1, 2, 0)


def solution(mesh):
    return jax.shard_map(
        local,
        mesh=mesh,
        in_specs=(
            P(None, None, "grp", "blk", None),
            P(None, "grp", "blk", None),
            P("grp", "blk", None),
            P("grp", "blk", None),
            P(),
        ),
        out_specs=P(None, "grp", "blk"),
        check_vma=False,
    )
```

time: 96.6 us -> 48.5 us (0.50)
  the two profiles are of different devices: /device:TPU:1 before, /device:TPU:8 now
where the time goes in v1:
time: 48.5 us; the launch traced here: 48.3 us
  Pallas kernels  43.4 us (89%)
  local copies, waits for them, and re-layouts  4.84 us (10%)
    pallas_call x1, Pallas kernels, local(): pl.pallas_call(functools.partial(kernel, norm), out_shape=jax.ShapeDtypeS...  43.4 us
    unnamed x10, local copies, waits for them, and re-layouts  4.14 us

profile of v1, /device:TPU:8, one launch (start us, length us, event | category | flops | bytes accessed | tf_op | source)
XLA Modules:
  0.0 48.3 jit_solution(15299716480590606222)
XLA Ops:
  0.0 0.0 copy-start
  0.0 1.4 %copy-done = bf16[3,256,2,4,128]{4,3,2,1,0:T(4,128)(2,1)S(1)} copy-done((bf16[3,256,2,4,128]{4,3,2,1,0:T(4,128)(2,1)S(1)}, bf16[3,256,2,4,128]{4,3,2,1,0:T(4,128)(2,1)}, u32[]{:S(2)}) %copy-start) | copy-done | bytes 1572888
  1.4 0.0 copy-start.1
  1.4 0.7 %copy-done.1 = f32[3,2,4,128]{3,2,1,0:T(4,128)S(1)} copy-done((f32[3,2,4,128]{3,2,1,0:T(4,128)S(1)}, f32[3,2,4,128]{3,2,1,0:T(4,128)}, u32[]{:S(2)}) %copy-start.1) | copy-done | bytes 12312
  2.1 0.0 copy-start.2
  2.1 0.7 %copy-done.2 = s32[2,4,128]{2,1,0:T(4,128)S(1)} copy-done((s32[2,4,128]{2,1,0:T(4,128)S(1)}, s32[2,4,128]{2,1,0:T(4,128)}, u32[]{:S(2)}) %copy-start.2) | copy-done | bytes 4120
  2.8 0.0 copy-start.3
  2.8 0.7 %copy-done.3 = s32[2,4,128]{2,1,0:T(4,128)S(1)} copy-done((s32[2,4,128]{2,1,0:T(4,128)S(1)}, s32[2,4,128]{2,1,0:T(4,128)}, u32[]{:S(2)}) %copy-start.3) | copy-done | bytes 4120
  3.5 0.0 copy-start.4
  3.5 0.7 %copy-done.4 = f32[16]{0:T(128)S(1)} copy-done((f32[16]{0:T(128)S(1)}, f32[16]{0:T(128)}, u32[]{:S(2)}) %copy-start.4) | copy-done | bytes 88
  4.1 43.4 %shard_map.55 = f32[8,128]{1,0:T(8,128)S(1)} custom-call(bf16[3,2048,128]{2,1,0:T(8,128)(2,1)S(1)} %bitcast.7, f32[24,128]{1,0:T(8,128)S(1)} %bitcast.8, s32[8,128]{1,0:T(8,128)S(1)} %bitcast.9, s32[8,128]{1,0:T(8,128)S(1)} %bitcast.10, f32[16]{0:T(128)S(1)} %copy-done.4), custom_call_target="tpu_custom_call" | custom-call | flops 3221225472 | bytes 2097152 | tf_op jit(solution)/shard_map/pallas_call | solution.py:346
  47.6 0.1 reshape.19
  47.6 0.6 %copy.8 = f32[8,8,16]{2,0,1:T(8,128)} copy(f32[8,8,16]{2,1,0:T(8,128)S(1)} %reshape.19) | data formatting | bytes 8192 | tf_op jit(solution)/shard_map/reshape | solution.py:365
Async XLA Ops:
  0.0 1.4 %copy-start = (bf16[3,256,2,4,128]{4,3,2,1,0:T(4,128)(2,1)S(1)}, bf16[3,256,2,4,128]{4,3,2,1,0:T(4,128)(2,1)}, u32[]{:S(2)}) copy-start(bf16[3,256,2,4,128]{4,3,2,1,0:T(4,128)(2,1)} %param.5) | copy-start | bytes 4718596
  1.4 0.7 %copy-start.1 = (f32[3,2,4,128]{3,2,1,0:T(4,128)S(1)}, f32[3,2,4,128]{3,2,1,0:T(4,128)}, u32[]{:S(2)}) copy-start(f32[3,2,4,128]{3,2,1,0:T(4,128)} %param.6) | copy-start | bytes 36868
  2.1 0.7 %copy-start.2 = (s32[2,4,128]{2,1,0:T(4,128)S(1)}, s32[2,4,128]{2,1,0:T(4,128)}, u32[]{:S(2)}) copy-start(s32[2,4,128]{2,1,0:T(4,128)} %param.7) | copy-start | bytes 12292
  2.8 0.7 %copy-start.3 = (s32[2,4,128]{2,1,0:T(4,128)S(1)}, s32[2,4,128]{2,1,0:T(4,128)}, u32[]{:S(2)}) copy-start(s32[2,4,128]{2,1,0:T(4,128)} %param.8) | copy-start | bytes 12292
  3.5 0.7 %copy-start.4 = (f32[16]{0:T(128)S(1)}, f32[16]{0:T(128)}, u32[]{:S(2)}) copy-start(f32[16]{0:T(128)} %scale_ref.1) | copy-start | bytes 196

commit v2 on v1

--- a/solution.py
+++ b/solution.py
@@ -13,17 +13,18 @@
 NX, NY = 2, 4
 F32, BF16 = jnp.float32, jnp.bfloat16
 MESH = pl.DeviceIdType.MESH
-BLOCKS = 4
+Z_OF = ((4, 3), (5, 2), (6, 7), (1, 0))
+BLOCKS = len(Z_OF)
 
 
 def kernel(
     norm,
     modes_hbm, metric_hbm, map_hbm, flags_hbm, scale_ref,
     out_ref,
-    nat, natf, slab, slabf, met, bmap, flg, gtab, bmat, pacc,
+    nat, natf, slab, slabf, met, bmap, flg, gtab, bmat, first, rest, pacc,
     hx_send, hy_send, hx_recv, hy_recv,
-    c_send, c_recv, x_send, x_recv, y_send, y_recv, z_send, z_recv, own,
-    in_sem, h_ssem, h_rsem, c_ssem, c_rsem, x_ssem, x_rsem, y_ssem, y_rsem, z_ssem, z_rsem,
+    c_send, c_recv, x_send, x_recv, z_send, z_recv,
+    in_sem, h_ssem, h_rsem, c_ssem, c_rsem, x_ssem, x_rsem, z_ssem, z_rsem,
 ):
     grp = lax.axis_index("grp")
     blk = lax.axis_index("blk")
@@ -41,12 +42,12 @@
         (grp, (blk + 1) % 32),
         (grp, (blk + 31) % 32),
     ]
-    yrel = [(s, t) for s in range(4) for t in range(2)]
+    x_rel = [(r, t) for r in range(4) for t in range(2)]
+    z_rel = [(q, s) for q in range(8) for s in range(4)]
     partners = list(halo_to)
     partners.append(at(dc=1))
-    partners += [at(dx=r) for r in range(1, 4)]
-    partners += [at(dyh=s, dyl=t) for s, t in yrel[1:]]
-    partners += [at(dz=q) for q in range(1, 8)]
+    partners += [at(dx=r, dyl=t) for r, t in x_rel[1:]]
+    partners += [at(dz=q, dyh=s) for q, s in z_rel[1:]]
 
     barrier = pltpu.get_barrier_semaphore()
     for p in partners:
@@ -133,7 +134,7 @@
                     both = jnp.concatenate(
                         [natf[d, pl.ds(st + row, 8, stride=CELLS), :] for st in starts], 0
                     )
-                    col = (row // 2) * 768 + d * 256 + (row % 2) * 128
+                    col = ((d + 1) % 3 * CELLS + row) * 128
                     bmat[rows, col:col + 128] = both.astype(BF16)
         return 0
 
@@ -151,6 +152,35 @@
             after = jnp.where(lane == 127, F32(0.0), pltpu.roll(v, 127, 1))
             before = jnp.where(lane == 0, F32(0.0), pltpu.roll(v, 1, 1))
             put(2, c, row, after - before)
+
+    def fill(ref, b, col, d, row):
+        bases = []
+        for t in range(2):
+            for q in Z_OF[b]:
+                bases.append((((y_lo + t) % 2) * 8 + (z + q) % 8) * (16 * CELLS))
+        a = [
+            jnp.concatenate(
+                [natf[c, pl.ds(st + row, 16, stride=CELLS), :] for st in bases], 0
+            )
+            for c in range(3)
+        ]
+        for k in range(KS):
+            g = [gtab[row, (d * 3 + c) * KS + k:(d * 3 + c) * KS + k + 1, :] for c in range(3)]
+            tested = (a[0] * g[0] + a[1] * g[1] + a[2] * g[2]).astype(BF16)
+            for p in range(4):
+                to = p * 128 + k * 16
+                ref[b, to:to + 16, col:col + 128] = tested[p * 16:p * 16 + 16]
+
+    def times(cols, tested):
+        return lax.dot_general(
+            bmat[:, cols], tested, (((1,), (1,)), ((), ())), preferred_element_type=F32
+        )
+
+    for b in range(BLOCKS):
+        for row in range(CELLS):
+            fill(first, b, row * 128, 2, row)
+    for b in range(BLOCKS):
+        pacc[b] = times(slice(0, 1024), first[b])
 
     for h in halo:
         h.wait_recv()
@@ -181,123 +211,82 @@
                 lo = s[c, row - 1] if yi > 0 else ys[0][xi]
                 put(1, c, row, hi - lo)
 
-    def compute(b):
-        bases = []
-        for t in range(2):
-            for e in range(2):
-                g = ((y_lo + t) % 2) * 8 + (z + 2 * b + e) % 8
-                bases.append(g * (16 * CELLS))
-
-        def rows_of(pair, d):
-            halves = []
-            for e in range(2):
-                row = pair * 2 + e
-                a = [
-                    [natf[c, pl.ds(st + row, 16, stride=CELLS), :] for st in bases]
-                    for c in range(3)
-                ]
-                a = [jnp.concatenate(v, 0) for v in a]
-                per_k = []
-                for k in range(KS):
-                    g = [gtab[row, pl.ds((d * 3 + c) * KS + k, 1), :] for c in range(3)]
-                    per_k.append((a[0] * g[0] + a[1] * g[1] + a[2] * g[2]).astype(BF16))
-                halves.append(
-                    jnp.concatenate(
-                        [per_k[k][p * 16:p * 16 + 16] for p in range(4) for k in range(KS)], 0
-                    )
-                )
-            return jnp.concatenate(halves, 1)
-
-        def step(pair, _):
-            total = None
-            for d in range(3):
-                tested = rows_of(pair, d)
-                cols = pl.ds(pl.multiple_of(pair * 768 + d * 256, 256), 256)
-                part = lax.dot_general(
-                    bmat[:, cols], tested, (((1,), (1,)), ((), ())),
-                    preferred_element_type=F32,
-                )
-                total = part if total is None else total + part
-            pacc[b] = total + pacc[b]
-            return 0
-
-        pacc[b] = jnp.zeros((M, 512), F32)
-        lax.fori_loop(0, 4, step, 0)
-
-    sent = []
-
-    def send(*args):
-        c = remote(*args)
-        c.start()
-        sent.append(c)
+    def fill_rest(b):
+        for d in range(2):
+            for row in range(CELLS):
+                fill(rest, b, (d * CELLS + row) * 128, d, row)
+
+    def remote_to(src, dst, ssem, rsem, **rel):
+        remote(src, dst, ssem, rsem, at(**rel)).start()
+
+    def done(ref, sem):
+        pltpu.make_async_copy(ref, ref, sem).wait()
 
     def send_core(b):
         c_send[b] = pacc[b, 128:256, :].astype(BF16)
-        send(c_send.at[b], c_recv.at[b], c_ssem.at[b], c_rsem.at[b], at(dc=1))
-
-    def arrived(dst, sem):
-        pltpu.make_async_copy(dst, dst, sem).wait()
+        remote_to(c_send.at[b], c_recv.at[b], c_ssem.at[b], c_rsem.at[b], dc=1)
 
     def send_x(b):
-        arrived(c_recv.at[b], c_rsem.at[b])
-        for r in (2, 1, 3, 0):
-            rows = slice(r * 32, r * 32 + 32)
-            v = pacc[b, rows, :] + c_recv[b, rows, :].astype(F32)
-            if r == 0:
-                pacc[b, rows, :] = v
+        done(c_recv.at[b], c_rsem.at[b])
+        for r, t in sorted(x_rel, key=lambda p: -(p[0] == 2) * 2 - (p[0] > 0) - p[1]):
+            rows, cols = slice(r * 32, r * 32 + 32), slice(t * 256, t * 256 + 256)
+            v = pacc[b, rows, cols] + c_recv[b, rows, cols].astype(F32)
+            n = (r * 2 + t) * 32
+            if n == 0:
+                pacc[b, rows, cols] = v
             else:
-                x_send[b, r] = v.astype(BF16)
-                send(x_send.at[b, r], x_recv.at[b, r], x_ssem.at[b, r], x_rsem.at[b, r], at(dx=r))
-
-    def send_y(b):
-        v = pacc[b, 0:32, :]
-        for r in range(1, 4):
-            arrived(x_recv.at[b, r], x_rsem.at[b, r])
-            v = v + x_recv[b, r].astype(F32)
-        for n, (sy, t) in reversed(list(enumerate(yrel))):
-            two = [v[sy * 8:sy * 8 + 8, t * 256 + e * 128:t * 256 + e * 128 + 128] for e in range(2)]
-            both = jnp.concatenate(two, 0)
-            if n == 0:
-                own[b] = both
-            else:
-                y_send[b, n] = both.astype(BF16)
-                send(
-                    y_send.at[b, n], y_recv.at[b, n], y_ssem.at[b, n], y_rsem.at[b, n],
-                    at(dyh=sy, dyl=t),
+                x_send[b, n:n + 32, :] = v.astype(BF16)
+                part = pl.ds(n, 32)
+                remote_to(
+                    x_send.at[b, part], x_recv.at[b, part], x_ssem.at[b], x_rsem.at[b],
+                    dx=r, dyl=t,
                 )
 
     def send_z(b):
-        v = own[b]
+        done(x_recv.at[b, pl.ds(32, 224)], x_rsem.at[b])
+        v = pacc[b, 0:32, 0:256]
         for n in range(1, 8):
-            arrived(y_recv.at[b, n], y_rsem.at[b, n])
-            v = v + y_recv[b, n].astype(F32)
+            v = v + x_recv[b, n * 32:n * 32 + 32, :].astype(F32)
         for e in range(2):
-            q = 2 * b + e
-            z_send[q] = v[e * 8:e * 8 + 8]
-            if q:
-                send(z_send.at[q], z_recv.at[q], z_ssem.at[q], z_rsem.at[q], at(dz=q))
-
-    for b in range(BLOCKS + 3):
+            for sy in (2, 1, 3, 0):
+                n = (e * 4 + 3 - sy) * 8
+                z_send[b, n:n + 8, :] = v[sy * 8:sy * 8 + 8, e * 128:e * 128 + 128]
+                if Z_OF[b][e] or sy:
+                    part = pl.ds(n, 8)
+                    remote_to(
+                        z_send.at[b, part], z_recv.at[b, part], z_ssem.at[b], z_rsem.at[b],
+                        dz=Z_OF[b][e], dyh=sy,
+                    )
+
+    fill_rest(0)
+    for b in range(BLOCKS + 2):
+        if b + 1 < BLOCKS:
+            fill_rest(b + 1)
         if b < BLOCKS:
-            compute(b)
+            pacc[b] = pacc[b] + times(slice(1024, 3072), rest[b])
             send_core(b)
         if 0 <= b - 1 < BLOCKS:
             send_x(b - 1)
         if 0 <= b - 2 < BLOCKS:
-            send_y(b - 2)
-        if 0 <= b - 3 < BLOCKS:
-            send_z(b - 3)
-
-    v = z_send[0]
-    for q in range(1, 8):
-        arrived(z_recv.at[q], z_rsem.at[q])
-        v = v + z_recv[q]
+            send_z(b - 2)
+
+    last = BLOCKS - 1
+    v = z_send[last, 56:64, :]
+    for b in range(BLOCKS):
+        if b == last:
+            done(z_recv.at[b, pl.ds(0, 56)], z_rsem.at[b])
+        else:
+            done(z_recv.at[b], z_rsem.at[b])
+        for n in range(7 if b == last else 8):
+            v = v + z_recv[b, n * 8:n * 8 + 8, :]
     out_ref[...] = v
 
     for h in halo:
         h.wait_send()
-    for c in sent:
-        c.wait_send()
+    for b in range(BLOCKS):
+        done(c_send.at[b], c_ssem.at[b])
+        done(x_send.at[b, pl.ds(32, 224)], x_ssem.at[b])
+        done(z_send.at[b, pl.ds(0, 56 if b == last else 64)], z_ssem.at[b])
 
 
 def local(modes, metric, block_map, flags, region_scale):
@@ -317,6 +306,8 @@
         pltpu.VMEM((CELLS, 128), jnp.int32),
         pltpu.VMEM((CELLS, 9 * KS, 128), F32),
         pltpu.VMEM((M, 3072), BF16),
+        pltpu.VMEM((BLOCKS, 512, 1024), BF16),
+        pltpu.VMEM((BLOCKS, 512, 2048), BF16),
         pltpu.VMEM((BLOCKS, M, 512), F32),
         pltpu.VMEM((2, 96, 128), BF16),
         pltpu.VMEM((2, 48, 128), BF16),
@@ -324,24 +315,19 @@
         pltpu.VMEM((2, 48, 128), BF16),
         pltpu.VMEM((BLOCKS, 128, 512), BF16),
         pltpu.VMEM((BLOCKS, 128, 512), BF16),
-        pltpu.VMEM((BLOCKS, 4, 32, 512), BF16),
-        pltpu.VMEM((BLOCKS, 4, 32, 512), BF16),
-        pltpu.VMEM((BLOCKS, 8, 16, 128), BF16),
-        pltpu.VMEM((BLOCKS, 8, 16, 128), BF16),
-        pltpu.VMEM((8, 8, 128), F32),
-        pltpu.VMEM((8, 8, 128), F32),
-        pltpu.VMEM((BLOCKS, 16, 128), F32),
+        pltpu.VMEM((BLOCKS, 256, 256), BF16),
+        pltpu.VMEM((BLOCKS, 256, 256), BF16),
+        pltpu.VMEM((BLOCKS, 64, 128), F32),
+        pltpu.VMEM((BLOCKS, 64, 128), F32),
         dma((5,)),
         dma((4,)),
         dma((4,)),
         dma((BLOCKS,)),
         dma((BLOCKS,)),
-        dma((BLOCKS, 4)),
-        dma((BLOCKS, 4)),
-        dma((BLOCKS, 8)),
-        dma((BLOCKS, 8)),
-        dma((8,)),
-        dma((8,)),
+        dma((BLOCKS,)),
+        dma((BLOCKS,)),
+        dma((BLOCKS,)),
+        dma((BLOCKS,)),
     ]
     summed = pl.pallas_call(
         functools.partial(kernel, norm),
@@ -350,7 +336,7 @@
         out_specs=pl.BlockSpec(memory_space=pltpu.VMEM),
         scratch_shapes=scratch,
         compiler_params=pltpu.CompilerParams(
-            collective_id=0, has_side_effects=True, vmem_limit_bytes=40 * 1024 * 1024
+            collective_id=0, has_side_effects=True, vmem_limit_bytes=63 * 1024 * 1024
         ),
         cost_estimate=pl.CostEstimate(
             flops=2 * 2048 * 3072 * 256, bytes_accessed=2 * 1024 * 1024, transcendentals=0

time: 48.5 us -> 42.5 us (0.88)
  the two profiles are of different devices: /device:TPU:8 before, /device:TPU:1 now
where the time goes in v2:
time: 42.5 us; the launch traced here: 42.2 us
  Pallas kernels  40.8 us (96%)
  local copies, waits for them, and re-layouts  1.38 us (3%)
    pallas_call x1, Pallas kernels, local(): pl.pallas_call(functools.partial(kernel, norm), out_shape=jax.ShapeDtypeS...  40.8 us
    reshape x2, local copies, waits for them, and re-layouts, local(): return summed.reshape(8, KS, 16).transpose(1, 2, 0)  1.38 us

profile of v2, /device:TPU:1, one launch (start us, length us, event | category | flops | bytes accessed | tf_op | source)
XLA Modules:
  0.0 42.2 jit_solution(11633083793268531314)
XLA Ops:
  0.0 40.8 %shard_map.55 = f32[8,128]{1,0:T(8,128)} custom-call(bf16[3,2048,128]{2,1,0:T(8,128)(2,1)} %bitcast.7, f32[24,128]{1,0:T(8,128)} %bitcast.8, s32[8,128]{1,0:T(8,128)} %bitcast.9, s32[8,128]{1,0:T(8,128)} %bitcast.10, f32[16]{0:T(128)} %scale_ref.1), custom_call_target="tpu_custom_call" | custom-call | flops 3221225472 | bytes 2097152 | tf_op jit(solution)/shard_map/pallas_call | solution.py:332
  40.8 0.8 %reshape.19 = f32[8,8,16]{2,1,0:T(8,128)S(1)} reshape(f32[8,128]{1,0:T(8,128)} %shard_map.55) | data formatting | bytes 8192 | tf_op jit(solution)/shard_map/reshape | solution.py:351
  41.6 0.6 %copy.8 = f32[8,8,16]{2,0,1:T(8,128)} copy(f32[8,8,16]{2,1,0:T(8,128)S(1)} %reshape.19) | data formatting | bytes 8192 | tf_op jit(solution)/shard_map/reshape | solution.py:351

commit v3 on v2

--- a/solution.py
+++ b/solution.py
@@ -134,7 +134,10 @@
                     both = jnp.concatenate(
                         [natf[d, pl.ds(st + row, 8, stride=CELLS), :] for st in starts], 0
                     )
-                    col = ((d + 1) % 3 * CELLS + row) * 128
+                    if d == 2:
+                        col = row * 128
+                    else:
+                        col = 1024 + (row // 2) * 512 + d * 256 + (row % 2) * 128
                     bmat[rows, col:col + 128] = both.astype(BF16)
         return 0
 
@@ -153,23 +156,46 @@
             before = jnp.where(lane == 0, F32(0.0), pltpu.roll(v, 1, 1))
             put(2, c, row, after - before)
 
-    def fill(ref, b, col, d, row):
+    wide = [256 * len(qs) for qs in Z_OF]
+
+    def tested(b, ds, pair):
         bases = []
         for t in range(2):
             for q in Z_OF[b]:
                 bases.append((((y_lo + t) % 2) * 8 + (z + q) % 8) * (16 * CELLS))
-        a = [
-            jnp.concatenate(
-                [natf[c, pl.ds(st + row, 16, stride=CELLS), :] for st in bases], 0
-            )
-            for c in range(3)
-        ]
-        for k in range(KS):
-            g = [gtab[row, (d * 3 + c) * KS + k:(d * 3 + c) * KS + k + 1, :] for c in range(3)]
-            tested = (a[0] * g[0] + a[1] * g[1] + a[2] * g[2]).astype(BF16)
-            for p in range(4):
-                to = p * 128 + k * 16
-                ref[b, to:to + 16, col:col + 128] = tested[p * 16:p * 16 + 16]
+
+        def rows_of(d):
+            halves = []
+            for e in range(2):
+                row = pair * 2 + e
+                a = [
+                    jnp.concatenate(
+                        [natf[c, pl.ds(st + row, 16, stride=CELLS), :] for st in bases], 0
+                    )
+                    for c in range(3)
+                ]
+                per_k = []
+                for k in range(KS):
+                    g = [gtab[row, pl.ds((d * 3 + c) * KS + k, 1), :] for c in range(3)]
+                    per_k.append((a[0] * g[0] + a[1] * g[1] + a[2] * g[2]).astype(BF16))
+                halves.append(
+                    jnp.concatenate(
+                        [
+                            per_k[k][p * 16:p * 16 + 16]
+                            for p in range(len(bases))
+                            for k in range(KS)
+                        ],
+                        0,
+                    )
+                )
+            return jnp.concatenate(halves, 1)
+
+        return jnp.concatenate([rows_of(d) for d in ds], 1)
+
+    def fill(ref, b, ds):
+        width = 256 * len(ds)
+        for pair in range(4):
+            ref[b, 0:wide[b], pair * width:pair * width + width] = tested(b, ds, pair)
 
     def times(cols, tested):
         return lax.dot_general(
@@ -177,10 +203,8 @@
         )
 
     for b in range(BLOCKS):
-        for row in range(CELLS):
-            fill(first, b, row * 128, 2, row)
-    for b in range(BLOCKS):
-        pacc[b] = times(slice(0, 1024), first[b])
+        fill(first, b, (2,))
+        pacc[b, :, 0:wide[b]] = times(slice(0, 1024), first[b, 0:wide[b], :])
 
     for h in halo:
         h.wait_recv()
@@ -211,82 +235,84 @@
                 lo = s[c, row - 1] if yi > 0 else ys[0][xi]
                 put(1, c, row, hi - lo)
 
-    def fill_rest(b):
-        for d in range(2):
-            for row in range(CELLS):
-                fill(rest, b, (d * CELLS + row) * 128, d, row)
-
     def remote_to(src, dst, ssem, rsem, **rel):
         remote(src, dst, ssem, rsem, at(**rel)).start()
 
     def done(ref, sem):
         pltpu.make_async_copy(ref, ref, sem).wait()
 
+    def core_part(ref, b):
+        return ref.at[b, :, pl.ds(0, wide[b])]
+
+    def x_part(ref, b, n=1, count=7):
+        return ref.at[b, pl.ds(n * 32, count * 32), pl.ds(0, wide[b] // 2)]
+
+    def z_part(ref, b, n, count):
+        return ref.at[b, pl.ds(n * 8, count * 8)]
+
     def send_core(b):
-        c_send[b] = pacc[b, 128:256, :].astype(BF16)
-        remote_to(c_send.at[b], c_recv.at[b], c_ssem.at[b], c_rsem.at[b], dc=1)
+        w = wide[b]
+        c_send[b, :, 0:w] = pacc[b, 128:256, 0:w].astype(BF16)
+        remote_to(core_part(c_send, b), core_part(c_recv, b), c_ssem.at[b], c_rsem.at[b], dc=1)
 
     def send_x(b):
-        done(c_recv.at[b], c_rsem.at[b])
-        for r, t in sorted(x_rel, key=lambda p: -(p[0] == 2) * 2 - (p[0] > 0) - p[1]):
-            rows, cols = slice(r * 32, r * 32 + 32), slice(t * 256, t * 256 + 256)
+        done(core_part(c_recv, b), c_rsem.at[b])
+        h = wide[b] // 2
+        for r, t in ((2, 1), (2, 0), (1, 1), (3, 1), (1, 0), (3, 0), (0, 1), (0, 0)):
+            rows, cols = slice(r * 32, r * 32 + 32), slice(t * h, t * h + h)
             v = pacc[b, rows, cols] + c_recv[b, rows, cols].astype(F32)
-            n = (r * 2 + t) * 32
+            n = r * 2 + t
             if n == 0:
                 pacc[b, rows, cols] = v
             else:
-                x_send[b, n:n + 32, :] = v.astype(BF16)
-                part = pl.ds(n, 32)
+                x_send[b, n * 32:n * 32 + 32, 0:h] = v.astype(BF16)
                 remote_to(
-                    x_send.at[b, part], x_recv.at[b, part], x_ssem.at[b], x_rsem.at[b],
+                    x_part(x_send, b, n, 1), x_part(x_recv, b, n, 1), x_ssem.at[b], x_rsem.at[b],
                     dx=r, dyl=t,
                 )
 
     def send_z(b):
-        done(x_recv.at[b, pl.ds(32, 224)], x_rsem.at[b])
-        v = pacc[b, 0:32, 0:256]
+        done(x_part(x_recv, b), x_rsem.at[b])
+        h = wide[b] // 2
+        v = pacc[b, 0:32, 0:h]
         for n in range(1, 8):
-            v = v + x_recv[b, n * 32:n * 32 + 32, :].astype(F32)
-        for e in range(2):
+            v = v + x_recv[b, n * 32:n * 32 + 32, 0:h].astype(F32)
+        for e, q in enumerate(Z_OF[b]):
             for sy in (2, 1, 3, 0):
-                n = (e * 4 + 3 - sy) * 8
-                z_send[b, n:n + 8, :] = v[sy * 8:sy * 8 + 8, e * 128:e * 128 + 128]
-                if Z_OF[b][e] or sy:
-                    part = pl.ds(n, 8)
+                n = e * 4 + 3 - sy
+                z_send[b, n * 8:n * 8 + 8, :] = v[sy * 8:sy * 8 + 8, e * 128:e * 128 + 128]
+                if q or sy:
                     remote_to(
-                        z_send.at[b, part], z_recv.at[b, part], z_ssem.at[b], z_rsem.at[b],
-                        dz=Z_OF[b][e], dyh=sy,
+                        z_part(z_send, b, n, 1), z_part(z_recv, b, n, 1), z_ssem.at[b], z_rsem.at[b],
+                        dz=q, dyh=sy,
                     )
 
-    fill_rest(0)
-    for b in range(BLOCKS + 2):
-        if b + 1 < BLOCKS:
-            fill_rest(b + 1)
-        if b < BLOCKS:
-            pacc[b] = pacc[b] + times(slice(1024, 3072), rest[b])
-            send_core(b)
-        if 0 <= b - 1 < BLOCKS:
+    for b in range(BLOCKS):
+        fill(rest, b, (0, 1))
+        w = wide[b]
+        pacc[b, :, 0:w] = pacc[b, :, 0:w] + times(slice(1024, 3072), rest[b, 0:w, :])
+        send_core(b)
+        if b:
             send_x(b - 1)
-        if 0 <= b - 2 < BLOCKS:
-            send_z(b - 2)
+    send_x(BLOCKS - 1)
+    for b in range(BLOCKS):
+        send_z(b)
 
     last = BLOCKS - 1
-    v = z_send[last, 56:64, :]
-    for b in range(BLOCKS):
-        if b == last:
-            done(z_recv.at[b, pl.ds(0, 56)], z_rsem.at[b])
-        else:
-            done(z_recv.at[b], z_rsem.at[b])
-        for n in range(7 if b == last else 8):
+    got = [4 * len(qs) - (b == last) for b, qs in enumerate(Z_OF)]
+    v = z_send[last, got[last] * 8:got[last] * 8 + 8, :]
+    for b in range(BLOCKS):
+        done(z_part(z_recv, b, 0, got[b]), z_rsem.at[b])
+        for n in range(got[b]):
             v = v + z_recv[b, n * 8:n * 8 + 8, :]
     out_ref[...] = v
 
     for h in halo:
         h.wait_send()
     for b in range(BLOCKS):
-        done(c_send.at[b], c_ssem.at[b])
-        done(x_send.at[b, pl.ds(32, 224)], x_ssem.at[b])
-        done(z_send.at[b, pl.ds(0, 56 if b == last else 64)], z_ssem.at[b])
+        done(core_part(c_send, b), c_ssem.at[b])
+        done(x_part(x_send, b), x_ssem.at[b])
+        done(z_part(z_send, b, 0, got[b]), z_ssem.at[b])
 
 
 def local(modes, metric, block_map, flags, region_scale):

time: 42.5 us -> 39 us (0.918)
  Pallas kernels: 40.8 us -> 37.5 us
    pallas_call x1, Pallas kernels: 40.8 us -> 37.5 us  [local(): pl.pallas_call(functools.partial(kernel, norm), out_shape=jax.ShapeDtypeS...]
where the time goes in v3:
time: 39 us; the launch traced here: 38.9 us
  Pallas kernels  37.5 us (96%)
  local copies, waits for them, and re-layouts  1.38 us (4%)
    pallas_call x1, Pallas kernels, local(): pl.pallas_call(functools.partial(kernel, norm), out_shape=jax.ShapeDtypeS...  37.5 us
    reshape x2, local copies, waits for them, and re-layouts, local(): return summed.reshape(8, KS, 16).transpose(1, 2, 0)  1.38 us

profile of v3, /device:TPU:1, one launch (start us, length us, event | category | flops | bytes accessed | tf_op | source)
XLA Modules:
  0.0 38.9 jit_solution(15153352996741219287)
XLA Ops:
  0.0 37.5 %shard_map.55 = f32[8,128]{1,0:T(8,128)} custom-call(bf16[3,2048,128]{2,1,0:T(8,128)(2,1)} %bitcast.7, f32[24,128]{1,0:T(8,128)} %bitcast.8, s32[8,128]{1,0:T(8,128)} %bitcast.9, s32[8,128]{1,0:T(8,128)} %bitcast.10, f32[16]{0:T(128)} %scale_ref.1), custom_call_target="tpu_custom_call" | custom-call | flops 3221225472 | bytes 2097152 | tf_op jit(solution)/shard_map/pallas_call | solution.py:358
  37.5 0.8 %reshape.19 = f32[8,8,16]{2,1,0:T(8,128)S(1)} reshape(f32[8,128]{1,0:T(8,128)} %shard_map.55) | data formatting | bytes 8192 | tf_op jit(solution)/shard_map/reshape | solution.py:377
  38.2 0.6 %copy.8 = f32[8,8,16]{2,0,1:T(8,128)} copy(f32[8,8,16]{2,1,0:T(8,128)S(1)} %reshape.19) | data formatting | bytes 8192 | tf_op jit(solution)/shard_map/reshape | solution.py:377

commit v4 on v3

--- a/solution.py
+++ b/solution.py
@@ -15,6 +15,9 @@
 MESH = pl.DeviceIdType.MESH
 Z_OF = ((4, 3), (5, 2), (6, 7), (1, 0))
 BLOCKS = len(Z_OF)
+INNER = tuple(((2, r), (2, r + 1), (1, r + 1 if r % 4 == 0 else r)) for r in (0, 2, 4, 6))
+OUTER = tuple(((0, r), (0, r + 1), (1, r if r % 4 == 0 else r + 1)) for r in (0, 2, 4, 6))
+ORDER = [dr for group in INNER + OUTER for dr in group]
 
 
 def kernel(
@@ -134,10 +137,7 @@
                     both = jnp.concatenate(
                         [natf[d, pl.ds(st + row, 8, stride=CELLS), :] for st in starts], 0
                     )
-                    if d == 2:
-                        col = row * 128
-                    else:
-                        col = 1024 + (row // 2) * 512 + d * 256 + (row % 2) * 128
+                    col = ORDER.index((d, row)) * 128
                     bmat[rows, col:col + 128] = both.astype(BF16)
         return 0
 
@@ -155,47 +155,42 @@
             after = jnp.where(lane == 127, F32(0.0), pltpu.roll(v, 127, 1))
             before = jnp.where(lane == 0, F32(0.0), pltpu.roll(v, 1, 1))
             put(2, c, row, after - before)
+            if row % NY in (1, 2):
+                put(1, c, row, s[c, row + 1] - s[c, row - 1])
 
     wide = [256 * len(qs) for qs in Z_OF]
 
-    def tested(b, ds, pair):
+    def tested(b, group):
         bases = []
         for t in range(2):
             for q in Z_OF[b]:
                 bases.append((((y_lo + t) % 2) * 8 + (z + q) % 8) * (16 * CELLS))
 
-        def rows_of(d):
-            halves = []
-            for e in range(2):
-                row = pair * 2 + e
-                a = [
-                    jnp.concatenate(
-                        [natf[c, pl.ds(st + row, 16, stride=CELLS), :] for st in bases], 0
-                    )
-                    for c in range(3)
-                ]
-                per_k = []
-                for k in range(KS):
-                    g = [gtab[row, pl.ds((d * 3 + c) * KS + k, 1), :] for c in range(3)]
-                    per_k.append((a[0] * g[0] + a[1] * g[1] + a[2] * g[2]).astype(BF16))
-                halves.append(
-                    jnp.concatenate(
-                        [
-                            per_k[k][p * 16:p * 16 + 16]
-                            for p in range(len(bases))
-                            for k in range(KS)
-                        ],
-                        0,
-                    )
+        def columns(d, row):
+            a = [
+                jnp.concatenate(
+                    [natf[c, pl.ds(st + row, 16, stride=CELLS), :] for st in bases], 0
                 )
-            return jnp.concatenate(halves, 1)
-
-        return jnp.concatenate([rows_of(d) for d in ds], 1)
-
-    def fill(ref, b, ds):
-        width = 256 * len(ds)
-        for pair in range(4):
-            ref[b, 0:wide[b], pair * width:pair * width + width] = tested(b, ds, pair)
+                for c in range(3)
+            ]
+            per_k = []
+            for k in range(KS):
+                g = [gtab[row, pl.ds((d * 3 + c) * KS + k, 1), :] for c in range(3)]
+                per_k.append((a[0] * g[0] + a[1] * g[1] + a[2] * g[2]).astype(BF16))
+            return jnp.concatenate(
+                [
+                    per_k[k][p * 16:p * 16 + 16]
+                    for p in range(len(bases))
+                    for k in range(KS)
+                ],
+                0,
+            )
+
+        return jnp.concatenate([columns(d, row) for d, row in group], 1)
+
+    def fill(ref, b, groups):
+        for n, group in enumerate(groups):
+            ref[b, 0:wide[b], n * 384:n * 384 + 384] = tested(b, group)
 
     def times(cols, tested):
         return lax.dot_general(
@@ -203,8 +198,8 @@
         )
 
     for b in range(BLOCKS):
-        fill(first, b, (2,))
-        pacc[b, :, 0:wide[b]] = times(slice(0, 1024), first[b, 0:wide[b], :])
+        fill(first, b, INNER)
+        pacc[b, :, 0:wide[b]] = times(slice(0, 1536), first[b, 0:wide[b], :])
 
     for h in halo:
         h.wait_recv()
@@ -231,9 +226,10 @@
                 hi = s[c, row + NY] if xi == 0 else xs[1][yi]
                 lo = s[c, row - NY] if xi == 1 else xs[0][yi]
                 put(0, c, row, hi - lo)
-                hi = s[c, row + 1] if yi < NY - 1 else ys[1][xi]
-                lo = s[c, row - 1] if yi > 0 else ys[0][xi]
-                put(1, c, row, hi - lo)
+                if yi == 0:
+                    put(1, c, row, s[c, row + 1] - ys[0][xi])
+                elif yi == NY - 1:
+                    put(1, c, row, ys[1][xi] - s[c, row - 1])
 
     def remote_to(src, dst, ssem, rsem, **rel):
         remote(src, dst, ssem, rsem, at(**rel)).start()
@@ -288,9 +284,9 @@
                     )
 
     for b in range(BLOCKS):
-        fill(rest, b, (0, 1))
+        fill(rest, b, OUTER)
         w = wide[b]
-        pacc[b, :, 0:w] = pacc[b, :, 0:w] + times(slice(1024, 3072), rest[b, 0:w, :])
+        pacc[b, :, 0:w] = pacc[b, :, 0:w] + times(slice(1536, 3072), rest[b, 0:w, :])
         send_core(b)
         if b:
             send_x(b - 1)
@@ -332,8 +328,8 @@
         pltpu.VMEM((CELLS, 128), jnp.int32),
         pltpu.VMEM((CELLS, 9 * KS, 128), F32),
         pltpu.VMEM((M, 3072), BF16),
-        pltpu.VMEM((BLOCKS, 512, 1024), BF16),
-        pltpu.VMEM((BLOCKS, 512, 2048), BF16),
+        pltpu.VMEM((BLOCKS, 512, 1536), BF16),
+        pltpu.VMEM((BLOCKS, 512, 1536), BF16),
         pltpu.VMEM((BLOCKS, M, 512), F32),
         pltpu.VMEM((2, 96, 128), BF16),
         pltpu.VMEM((2, 48, 128), BF16),

time: 39 us -> 38.5 us (0.987)
  Pallas kernels: 37.5 us -> 36.9 us
    pallas_call x1, Pallas kernels: 37.5 us -> 36.9 us  [local(): pl.pallas_call(functools.partial(kernel, norm), out_shape=jax.ShapeDtypeS...]
where the time goes in v4:
time: 38.5 us; the launch traced here: 38.3 us
  Pallas kernels  36.9 us (96%)
  local copies, waits for them, and re-layouts  1.38 us (4%)
    pallas_call x1, Pallas kernels, local(): pl.pallas_call(functools.partial(kernel, norm), out_shape=jax.ShapeDtypeS...  36.9 us
    reshape x2, local copies, waits for them, and re-layouts, local(): return summed.reshape(8, KS, 16).transpose(1, 2, 0)  1.38 us

profile of v4, /device:TPU:1, one launch (start us, length us, event | category | flops | bytes accessed | tf_op | source)
XLA Modules:
  0.0 38.3 jit_solution(7586695818919589532)
XLA Ops:
  0.0 36.9 %shard_map.55 = f32[8,128]{1,0:T(8,128)} custom-call(bf16[3,2048,128]{2,1,0:T(8,128)(2,1)} %bitcast.7, f32[24,128]{1,0:T(8,128)} %bitcast.8, s32[8,128]{1,0:T(8,128)} %bitcast.9, s32[8,128]{1,0:T(8,128)} %bitcast.10, f32[16]{0:T(128)} %scale_ref.1), custom_call_target="tpu_custom_call" | custom-call | flops 3221225472 | bytes 2097152 | tf_op jit(solution)/shard_map/pallas_call | solution.py:354
  36.9 0.8 %reshape.19 = f32[8,8,16]{2,1,0:T(8,128)S(1)} reshape(f32[8,128]{1,0:T(8,128)} %shard_map.55) | data formatting | bytes 8192 | tf_op jit(solution)/shard_map/reshape | solution.py:373
  37.7 0.6 %copy.8 = f32[8,8,16]{2,0,1:T(8,128)} copy(f32[8,8,16]{2,1,0:T(8,128)S(1)} %reshape.19) | data formatting | bytes 8192 | tf_op jit(solution)/shard_map/reshape | solution.py:373
